TPU v7x, 32 devices: a whole 2x2x4 slice. The times are simulated.
32 devices in a mesh: grp: 2 (over y), dp: 4 (over z), tensor: 4 (over x, core).
Axes of the slice: x: 2, y: 2, z: 4, core: 2. Of those that a mesh axis runs over, the one named last changes fastest.
Arguments:
- resid: bfloat16 [16, 2, 8192], P(('grp', 'dp'), None, 'tensor'), parts along dimension 0, may hold values from -6 to 6
- queries: bfloat16 [16, 2, 64, 128], P(('grp', 'dp'), None, 'tensor'), parts along dimension 0, may hold values from -12.5 to 12.5
- new_kv: bfloat16 [16, 3, 4, 2, 128], P(('grp', 'dp'), None, 'tensor'), parts along dimension 0, may hold values from -12.5 to 12.5
- tail_fill: int32 [16, 2], P(('grp', 'dp')), parts along dimension 0, may hold values from 1 to 16
- page_ids: int32 [16, 2, 4, 32], P(('grp', 'dp'), None, 'tensor'), parts along dimension 0, may hold values from 0 to 2559, as said below
- kv_pool: bfloat16 [5120, 2, 16, 128], P(('grp', 'dp', 'tensor')), parts along dimension 0, may hold values from -6 to 6
- norm_gain: float32 [8192], replicated, may hold values from 0.1 to 1.9
- gate_weight: bfloat16 [8192, 26624], P(None, ('dp', 'tensor')), may hold values from -0.0625 to 0.0625
- up_weight: bfloat16 [8192, 26624], P(None, ('dp', 'tensor')), may hold values from -0.0625 to 0.0625
- down_weight: bfloat16 [26624, 8192], P(('dp', 'tensor')), may hold values from -0.0390625 to 0.0390625
Outputs:
- attended: bfloat16 [16, 2, 8192], P(('grp', 'dp'), None, 'tensor'), parts along dimension 0
- ffn_out: bfloat16 [32, 8192], P(('grp', 'dp', 'tensor')), parts along dimension 0
There are 2 independent parts, one for each index of `grp`. A program takes and returns all parts, laid end to end along the dimension named above; an argument that names none is the same for every part. Nothing has to cross between parts.
Inputs may be any that keep to these rules, and one draw needn't show every extreme that they name: `page_ids`: for one dp index i and KV head g, the ids of rows i * 2 to (i + 1) * 2 - 1, all steps, head g are distinct; at most 16 of them lie in any one block of pool slots k * 160 to (k + 1) * 160 - 1, and in every draw some block holds exactly 16 of them for every such (i, g).
All inputs are finite; a program needn't handle non-finite values.
Results may differ from a plain program's by a relative error of at most 0.0081.
Values may be sent and summed in bfloat16 or wider, within the bound.
A program may use at most 192 MiB of HBM per device.

v0:
```python
import math

import jax
import jax.numpy as jnp
from jax import lax
from jax.sharding import PartitionSpec as P

PAGE = 16
SEL = 32


def attend_group(query_group, page_keys, page_values, fresh_keys, fresh_values, fill_count):
    score_scale = 1.0 / math.sqrt(query_group.shape[-1])
    page_scores = (
        jnp.einsum("rshd,rskd->rshk", query_group, page_keys, preferred_element_type=jnp.float32)
        * score_scale
    )
    fresh_scores = (
        jnp.einsum("rshd,rjd->rshj", query_group, fresh_keys, preferred_element_type=jnp.float32)
        * score_scale
    )
    key_index = jnp.arange(page_keys.shape[2], dtype=jnp.int32)
    page_valid = (key_index[None, None, :] >= PAGE) | (
        key_index[None, None, :] < fill_count[:, :, None]
    )
    page_scores = jnp.where(page_valid[:, :, None, :], page_scores, -jnp.inf)
    fresh_index = jnp.arange(fresh_keys.shape[1], dtype=jnp.int32)
    step_index = jnp.arange(fill_count.shape[1], dtype=jnp.int32)
    fresh_valid = fresh_index[None, :] <= step_index[:, None] + 1
    fresh_scores = jnp.where(fresh_valid[None, :, None, :], fresh_scores, -jnp.inf)
    top_score = jnp.maximum(jnp.max(page_scores, axis=-1), jnp.max(fresh_scores, axis=-1))
    page_exp = jnp.exp(page_scores - top_score[..., None])
    fresh_exp = jnp.exp(fresh_scores - top_score[..., None])
    total = jnp.sum(page_exp, axis=-1) + jnp.sum(fresh_exp, axis=-1)
    page_weights = (page_exp / total[..., None]).astype(jnp.bfloat16)
    fresh_weights = (fresh_exp / total[..., None]).astype(jnp.bfloat16)
    page_part = jnp.einsum(
        "rshk,rskd->rshd", page_weights, page_values, preferred_element_type=jnp.float32
    )
    fresh_part = jnp.einsum(
        "rshj,rjd->rshd", fresh_weights, fresh_values, preferred_element_type=jnp.float32
    )
    return page_part + fresh_part


def shards(
    resid,
    queries,
    new_kv,
    tail_fill,
    page_ids,
    kv_pool,
    norm_gain,
    gate_weight,
    up_weight,
    down_weight,
):
    owner_total = lax.axis_size("dp") * lax.axis_size("tensor")
    pool_slots = kv_pool.shape[0]
    row_count = resid.shape[0]
    step_count = resid.shape[1]
    slot_list = page_ids.reshape(-1)
    request_total = slot_list.shape[0]
    capacity = max(2, (2 * request_total + owner_total - 1) // owner_total)
    owner_list = slot_list // pool_slots
    local_list = slot_list % pool_slots
    owner_onehot = (
        owner_list[:, None] == jnp.arange(owner_total, dtype=jnp.int32)[None, :]
    ).astype(jnp.int32)
    order_rank = jnp.sum(jnp.cumsum(owner_onehot, axis=0) * owner_onehot, axis=1) - 1
    position = owner_list * capacity + order_rank
    request_buffer = jnp.zeros((owner_total * capacity,), jnp.int32).at[position].set(local_list)
    request_buffer = request_buffer.reshape(owner_total, capacity)
    returned = lax.all_to_all(
        kv_pool[
            lax.all_to_all(
                request_buffer, ("dp", "tensor"), split_axis=0, concat_axis=0, tiled=True
            )
        ],
        ("dp", "tensor"),
        split_axis=0,
        concat_axis=0,
        tiled=True,
    )
    page_rows = returned.reshape((owner_total * capacity,) + kv_pool.shape[1:])[position]
    page_rows = page_rows.reshape(row_count, step_count, SEL, 2, PAGE, kv_pool.shape[-1])
    page_keys = page_rows[:, :, :, 0].reshape(row_count, step_count, SEL * PAGE, kv_pool.shape[-1])
    page_values = page_rows[:, :, :, 1].reshape(
        row_count, step_count, SEL * PAGE, kv_pool.shape[-1]
    )
    fresh_pair = new_kv[:, :, 0]
    attn = attend_group(
        queries, page_keys, page_values, fresh_pair[:, :, 0], fresh_pair[:, :, 1], tail_fill
    )
    attn = attn.reshape(row_count, step_count, resid.shape[2])
    attended = (resid.astype(jnp.float32) + attn).astype(jnp.bfloat16)
    full_rows = lax.all_gather(attended, "tensor", axis=2, tiled=True).astype(jnp.float32)
    mean_square = jnp.mean(full_rows * full_rows, axis=-1, keepdims=True)
    normed = (full_rows * lax.rsqrt(mean_square + 1e-05) * norm_gain).astype(jnp.bfloat16)
    block_rows = lax.all_gather(normed, "dp", axis=0, tiled=True)
    flat_rows = block_rows.reshape(-1, block_rows.shape[-1])
    gate_act = jnp.dot(flat_rows, gate_weight, preferred_element_type=jnp.float32)
    up_act = jnp.dot(flat_rows, up_weight, preferred_element_type=jnp.float32)
    hidden_rows = (jax.nn.silu(gate_act) * up_act).astype(jnp.bfloat16)
    hidden_all = hidden_rows.reshape(block_rows.shape[0], block_rows.shape[1], -1)
    hidden_flat = hidden_all.reshape(-1, hidden_all.shape[-1])
    summed = lax.psum_scatter(
        jnp.dot(hidden_flat, down_weight, preferred_element_type=jnp.float32),
        ("dp", "tensor"),
        scatter_dimension=0,
        tiled=True,
    )
    ffn_out = summed.astype(jnp.bfloat16)
    return (attended, ffn_out)


def solution(mesh):
    return jax.shard_map(
        shards,
        mesh=mesh,
        in_specs=(
            P(("grp", "dp"), None, "tensor"),
            P(("grp", "dp"), None, "tensor", None),
            P(("grp", "dp"), None, "tensor", None, None),
            P(("grp", "dp"), None),
            P(("grp", "dp"), None, "tensor", None),
            P(("grp", "dp", "tensor"), None, None, None),
            P(),
            P(None, ("dp", "tensor")),
            P(None, ("dp", "tensor")),
            P(("dp", "tensor"), None),
        ),
        out_specs=(P(("grp", "dp"), None, "tensor"), P(("grp", "dp", "tensor"), None)),
        check_vma=False,
    )
```

profile of v0, /device:TPU:0, one launch (start us, length us, event | category | flops | bytes accessed | tf_op | source)
XLA Modules:
  0.0 191.7 jit_solution(1327179504672195280)
XLA Ops:
  0.6 0.0 copy-start
  0.6 0.8 and_reduce_fusion
  1.5 0.5 broadcast.213
  2.0 1.4 fusion.28
  3.3 0.1 div.47
  3.4 0.1 rem.30
  3.5 0.1 ne.57
  3.6 0.1 fusion.17
  3.7 0.2 reduce_window_sum.11
  3.9 0.2 select_reduce_fusion
  4.0 0.1 div.46
  4.1 0.1 and.24
  4.2 1.0 scatter_custom_fusion
  5.2 0.1 all_to_all.11
  5.3 13.6 %all_to_all.17 = s32[16,1,16]{2,1,0:T(1,128)S(1)} all-to-all(s32[16,1,16]{2,1,0:T(1,128)S(1)} %all_to_all.11), channel_id=1, replica_groups=mesh['grp'=2,'dp'=4,'tensor'=4] {'dp','tensor'}, dimensions={0} | all-to-all | bytes 2048 | tf_op jit(solution)/shard_map/all_to_all | solution.py:76
  18.9 0.1 reshape.198
  19.0 0.0 copy-done
  19.0 2.2 %gather_fusion = bf16[256,2,16,128]{3,2,1,0:T(8,128)(2,1)} fusion(bf16[160,2,16,128]{3,2,1,0:T(8,128)(2,1)S(1)} %copy-done, s32[1024]{0:T(1024)S(1)} %pad_clamp_fusion.1), kind=kCustom, calls=%fused_computation | custom fusion | bytes 4195328 | tf_op jit(solution)/shard_map/gather | solution.py:75
  21.2 3.7 %all-to-all-start.1 = ((bf16[16,16,2,16,128]{4,3,2,1,0:T(8,128)(2,1)}), bf16[16,16,2,16,128]{4,3,2,1,0:T(8,128)(2,1)S(1)}, u32[]{:S(2)}, u32[]{:S(2)}) async-start(bf16[16,16,2,16,128]{4,3,2,1,0:T(8,128)(2,1)} %bitcast.3), calls=%async_computation.1 | async-start | bytes 4194304 | tf_op jit(solution)/shard_map/all_to_all | solution.py:74
  24.9 0.7 copy.24
  25.6 1.2 dynamic-slice
  26.9 0.1 iota_compare_fusion.2
  26.9 0.8 compare_or_fusion
  27.7 0.9 fusion.31
  28.6 37.4 %all-to-all-done.1 = bf16[16,16,2,16,128]{4,3,2,1,0:T(8,128)(2,1)S(1)} async-done(((bf16[16,16,2,16,128]{4,3,2,1,0:T(8,128)(2,1)}), bf16[16,16,2,16,128]{4,3,2,1,0:T(8,128)(2,1)S(1)}, u32[]{:S(2)}, u32[]{:S(2)}) %all-to-all-start.1) | async-done | bytes 2097184 | tf_op jit(solution)/shard_map/all_to_all | solution.py:74
  65.9 0.8 gather_fusion.1
  66.7 0.2 fusion.29
  66.9 1.0 fusion.30
  68.0 0.2 fusion.8
  68.2 0.2 fusion.14
  68.4 0.2 convolution_add_fusion
  68.7 0.7 add_convert_fusion
  69.4 0.0 copy-start.2
  69.4 7.3 %all_gather.6 = bf16[2,2,8192]{2,1,0:T(2,128)(2,1)S(1)} all-gather(bf16[2,2,2048]{2,1,0:T(2,128)(2,1)S(1)} %add_convert_fusion), channel_id=1, replica_groups=mesh['grp'=2,'dp'=4,'tensor'=4] {'tensor'}, dimensions={2}, use_global_device_ids=true | all-gather | bytes 81920 | tf_op jit(solution)/shard_map/all_gather | solution.py:97
  76.8 0.2 fusion.5
  77.0 0.9 fusion.7
  77.9 18.8 %all_gather.7 = bf16[8,2,8192]{2,1,0:T(2,128)(2,1)S(1)} all-gather(bf16[2,2,8192]{2,1,0:T(2,128)(2,1)S(1)} %fusion.7), channel_id=1, replica_groups=mesh['grp'=2,'dp'=4,'tensor'=4] {'dp'}, dimensions={0}, use_global_device_ids=true | all-gather | bytes 327680 | tf_op jit(solution)/shard_map/all_gather | solution.py:100
  96.7 0.1 reshape.195
  96.8 0.0 copy-start.1
  96.8 10.7 %fusion.32 = f32[16,1664]{1,0:T(8,128)S(1)} fusion(bf16[16,8192]{1,0:T(8,128)(2,1)S(1)} %reshape.195, bf16[8192,1664]{1,0:T(8,128)(2,1)} %param.17), kind=kOutput, calls=%fused_computation.68 | convolution fusion | flops 436207616 | bytes 27631616 | tf_op jit(solution)/shard_map/dot_general | solution.py:102
  107.5 19.7 %fusion.1 = f32[16,8192]{1,0:T(8,128)S(1)} fusion(bf16[1664,8192]{1,0:T(8,128)(2,1)} %param.19, bf16[16,8192]{1,0:T(8,128)(2,1)S(1)} %reshape.195, bf16[8192,1664]{1,0:T(8,128)(2,1)} %param.18, f32[16,1664]{1,0:T(8,128)S(1)} %fusion.32), kind=kOutput, calls=%fused_computation.5 | convolution fusion | flops 872574976 | bytes 55418880 | tf_op jit(solution)/shard_map/dot_general | solution.py:108
  127.2 0.0 copy-done.2
  127.2 63.2 %all-reduce.2 = bf16[16,8192]{1,0:T(8,128)(2,1)S(1)} all-reduce(f32[16,8192]{1,0:T(8,128)S(1)} %fusion.1), channel_id=2, replica_groups=mesh['grp'=2,'dp'=4,'tensor'=4] {'dp','tensor'}, use_global_device_ids=true, to_apply=%region_8.9.clone | all-reduce | flops 131072 | bytes 786432
  190.4 1.3 dynamic-slice_convert_fusion
  191.7 0.0 copy-done.1
  (12 shorter events, 0.1 us)
Async XLA Ops:
  0.6 18.3 %copy-start = (bf16[160,2,16,128]{3,2,1,0:T(8,128)(2,1)S(1)}, bf16[160,2,16,128]{3,2,1,0:T(8,128)(2,1)}, u32[]{:S(2)}) copy-start(bf16[160,2,16,128]{3,2,1,0:T(8,128)(2,1)} %param.15) | copy-start | bytes 3932164
  21.2 44.8 %all-to-all-start.1 = ((bf16[16,16,2,16,128]{4,3,2,1,0:T(8,128)(2,1)}), bf16[16,16,2,16,128]{4,3,2,1,0:T(8,128)(2,1)S(1)}, u32[]{:S(2)}, u32[]{:S(2)}) async-start(bf16[16,16,2,16,128]{4,3,2,1,0:T(8,128)(2,1)} %bitcast.3), calls=%async_computation.1 | async-start | bytes 4194304 | tf_op jit(solution)/shard_map/all_to_all | solution.py:74
  69.4 57.8 %copy-start.2 = (bf16[2,2,2048]{2,1,0:T(2,128)(2,1)}, bf16[2,2,2048]{2,1,0:T(2,128)(2,1)S(1)}, u32[]{:S(2)}) copy-start(bf16[2,2,2048]{2,1,0:T(2,128)(2,1)S(1)} %add_convert_fusion) | copy-start | bytes 49156
  96.8 94.9 %copy-start.1 = (bf16[160,2,16,128]{3,2,1,0:T(8,128)(2,1)S(1)}, bf16[160,2,16,128]{3,2,1,0:T(8,128)(2,1)}, u32[]{:S(2)}) copy-start(bf16[160,2,16,128]{3,2,1,0:T(8,128)(2,1)} %param.15) | copy-start | bytes 3932164
where the time goes:
time: 192 us
  blocking collectives  103 us (54%)
  waiting for transfers between devices  37.4 us (19%)
  matrix products  32.8 us (17%)
  local copies, waits for them, and re-layouts  8.6 us (4%)
  other arithmetic  5.53 us (3%)
  starting transfers between devices  3.72 us (2%)
    unnamed x1, blocking collectives  63.2 us
    all_to_all x1, waiting for transfers between devices, shards(): lax.all_to_all(kv_pool[lax.all_to_all(request_buffer, ('dp', 'tensor'), s...  37.4 us
    dot_general x1, matrix products, shards(): jnp.dot(hidden_flat, down_weight, preferred_element_type=jnp.float32)  19.7 us
    all_gather x1, blocking collectives, shards(): block_rows = lax.all_gather(normed, 'dp', axis=0, tiled=True)  18.8 us
    all_to_all x1, blocking collectives, shards(): lax.all_to_all(request_buffer, ('dp', 'tensor'), split_axis=0, concat_axi...  13.6 us
    dot_general x1, matrix products, shards(): jnp.dot(flat_rows, gate_weight, preferred_element_type=jnp.float32)  10.7 us
    all_gather x1, blocking collectives, shards(): lax.all_gather(attended, 'tensor', axis=2, tiled=True).astype(jnp.float32)  7.33 us
  transfers between devices with their start and end apart: 1, of which 1 were waited for; matrix products, arithmetic and copies ran while one was open for 2% of the time, Pallas kernels for 0%

commit v1 on v0

--- a/solution.py
+++ b/solution.py
@@ -1,8 +1,11 @@
+import functools
 import math
 
 import jax
 import jax.numpy as jnp
 from jax import lax
+from jax.experimental import pallas as pl
+from jax.experimental.pallas import tpu as pltpu
 from jax.sharding import PartitionSpec as P
 
 PAGE = 16
@@ -114,22 +117,533 @@
     return (attended, ffn_out)
 
 
+def fits_fused(mesh, resid, queries, page_ids, kv_pool, gate_weight):
+    owners = mesh.shape["dp"] * mesh.shape["tensor"]
+    rows = resid.shape[0] // (mesh.shape["grp"] * mesh.shape["dp"])
+    steps = resid.shape[1]
+    wide = gate_weight.shape[1] // owners
+    return (
+        owners == 16
+        and rows * steps * mesh.shape["dp"] == owners
+        and (queries.shape[2] // mesh.shape["tensor"]) % 8 == 0
+        and rows * steps * (queries.shape[2] // mesh.shape["tensor"]) == 64
+        and rows * steps * page_ids.shape[3] == 128
+        and queries.shape[3] == 128
+        and wide % 128 == 0
+        and 4 * wide <= gate_weight.shape[0]
+        and gate_weight.shape[0] % 1024 == 0
+    )
+
+
+def fused_kernel(
+    dims,
+    q_ref,
+    meta_ref,
+    fresh_k_ref,
+    fresh_v_ref,
+    resid_ref,
+    gain_ref,
+    pool_hbm,
+    gate_hbm,
+    up_hbm,
+    down_hbm,
+    att_ref,
+    out_ref,
+    ring,
+    pool,
+    meta_all,
+    q_all,
+    o_send,
+    o_all,
+    ml_send,
+    ml_all,
+    x_all,
+    list_vmem,
+    list_smem,
+    code_ref,
+    y_ref,
+    x_ref,
+    h_ref,
+    part_ref,
+    p_send,
+    p_all,
+    pool_sem,
+    list_sem,
+    ring_sem,
+    send_sem,
+    meta_sem,
+    q_sem,
+    o_sem,
+    ml_sem,
+    x_sem,
+    p_sem,
+):
+    n_dp, n_tensor, slots, wide, depth, ring_slots, rows, steps, heads, sel = dims
+    owners = n_dp * n_tensor
+    dp = lax.axis_index("dp")
+    tensor = lax.axis_index("tensor")
+    me = dp * n_tensor + tensor
+    chunks = wide // 128
+    down_loads = depth // 1024
+    loads = chunks + down_loads
+    quer = rows * steps * heads
+    pages = rows * steps * sel
+
+    def gate_copies(load, slot):
+        column = pl.multiple_of(load * 128, 128)
+        return [
+            pltpu.make_async_copy(
+                source.at[:, pl.ds(column, 128)],
+                ring.at[slot, :, pl.ds(128 * half, 128)],
+                ring_sem.at[slot, half],
+            )
+            for half, source in ((0, gate_hbm), (1, up_hbm))
+        ]
+
+    def down_copies(load, slot):
+        return [
+            pltpu.make_async_copy(
+                down_hbm.at[:, pl.ds(pl.multiple_of(load * 1024 + 256 * q, 256), 256)],
+                ring.at[slot, pl.ds(q * wide, wide), :],
+                ring_sem.at[slot, q],
+            )
+            for q in range(4)
+        ]
+
+    pool_copy = pltpu.make_async_copy(pool_hbm, pool, pool_sem)
+    pool_copy.start()
+
+    def peer_of(offset):
+        peer = lax.rem(me + offset, owners)
+        return peer, {"dp": peer // n_tensor, "tensor": peer % n_tensor}
+
+    def remote(kind, source, target, sems, peer, device, index):
+        return pltpu.make_async_remote_copy(
+            src_ref=source,
+            dst_ref=target,
+            send_sem=send_sem.at[kind, peer],
+            recv_sem=sems.at[index],
+            device_id=device,
+            device_id_type=pl.DeviceIdType.MESH,
+        )
+
+    barrier = pltpu.get_barrier_semaphore()
+
+    def greet(offset, carry):
+        _, device = peer_of(offset)
+        pl.semaphore_signal(barrier, inc=1, device_id=device, device_id_type=pl.DeviceIdType.MESH)
+        return carry
+
+    lax.fori_loop(1, owners, greet, 0)
+
+    def preload(load, carry):
+        for copy in gate_copies(load, load):
+            copy.start()
+        return carry
+
+    lax.fori_loop(0, min(chunks, ring_slots), preload, 0)
+    for load in range(chunks, ring_slots):
+        for copy in down_copies(load - chunks, load):
+            copy.start()
+
+    pl.semaphore_wait(barrier, owners - 1)
+
+    def send_queries(offset, carry):
+        peer, device = peer_of(offset)
+        remote(0, meta_ref, meta_all.at[me], meta_sem, peer, device, me).start()
+        remote(1, q_ref, q_all.at[me], q_sem, peer, device, me).start()
+        return carry
+
+    lax.fori_loop(1, owners, send_queries, 0)
+    meta_all[me] = meta_ref[...]
+    q_all[me] = q_ref[...]
+
+    scale = 1.0 / math.sqrt(q_ref.shape[-1])
+    fresh_scores = (
+        lax.dot_general(
+            q_ref[...],
+            fresh_k_ref[...],
+            (((1,), (1,)), ((), ())),
+            preferred_element_type=jnp.float32,
+        )
+        * scale
+    )
+    qi = lax.broadcasted_iota(jnp.int32, fresh_scores.shape, 0)
+    fi = lax.broadcasted_iota(jnp.int32, fresh_scores.shape, 1)
+    fresh = steps + 1
+    fresh_ok = (fi // fresh == qi // (steps * heads)) & (
+        fi % fresh <= (qi // heads) % steps + 1
+    )
+    fresh_scores = jnp.where(fresh_ok, fresh_scores, -1e30)
+    fresh_top = jnp.max(fresh_scores, axis=1, keepdims=True)
+    fresh_exp = jnp.where(fresh_ok, jnp.exp(fresh_scores - fresh_top), 0.0)
+    fresh_total = jnp.sum(fresh_exp, axis=1, keepdims=True)
+    fresh_out = jnp.dot(
+        fresh_exp.astype(jnp.bfloat16), fresh_v_ref[...], preferred_element_type=jnp.float32
+    )
+
+    def as_rows(first, second):
+        lane = lax.broadcasted_iota(jnp.int32, (quer, 128), 1)
+        both = jnp.where(lane == 0, first, jnp.where(lane == 1, second, 0.0))
+        both = jnp.concatenate([both, jnp.zeros((128 - quer, 128), jnp.float32)], axis=0)
+        return jnp.transpose(both)[0:8]
+
+    fresh_rows = as_rows(fresh_top, fresh_total)
+
+    def wait_meta(offset, carry):
+        peer, device = peer_of(offset)
+        remote(0, meta_ref, meta_all.at[peer], meta_sem, peer, device, peer).wait_recv()
+        return carry
+
+    lax.fori_loop(1, owners, wait_meta, 0)
+
+    ids = meta_all[:, 0, :]
+    extra = meta_all[:, 1, :]
+    local = ids - me * slots
+    inside = (local >= 0) & (local < slots)
+    row_i = lax.broadcasted_iota(jnp.int32, (pages, pages), 0)
+    col_i = lax.broadcasted_iota(jnp.int32, (pages, pages), 1)
+    before = jnp.where(row_i < col_i, 1.0, 0.0).astype(jnp.bfloat16)
+    rank = jnp.dot(
+        jnp.where(inside, 1.0, 0.0).astype(jnp.bfloat16), before, preferred_element_type=jnp.float32
+    )
+    capacity = max(2, (2 * pages + owners - 1) // owners)
+    lane = lax.broadcasted_iota(jnp.int32, ids.shape, 1)
+    slot_list = jnp.zeros(ids.shape, jnp.float32)
+    code_list = jnp.zeros(ids.shape, jnp.float32)
+    local_float = local.astype(jnp.float32)
+    extra_float = extra.astype(jnp.float32)
+    for k in range(capacity):
+        chosen = inside & (rank == float(k))
+        slot_k = jnp.sum(jnp.where(chosen, local_float, 0.0), axis=1, keepdims=True)
+        code_k = jnp.sum(jnp.where(chosen, extra_float, 0.0), axis=1, keepdims=True)
+        slot_list = jnp.where(lane == k, slot_k, slot_list)
+        code_list = jnp.where(lane == k, code_k, code_list)
+    list_vmem[...] = slot_list.astype(jnp.int32)
+    list_copy = pltpu.make_async_copy(list_vmem, list_smem, list_sem)
+    list_copy.start()
+    keys = capacity * PAGE
+    spread_k = lax.broadcasted_iota(jnp.int32, (pages, keys), 0)
+    spread_c = lax.broadcasted_iota(jnp.int32, (pages, keys), 1)
+    spread = jnp.where(spread_c // PAGE == spread_k, 1.0, 0.0).astype(jnp.bfloat16)
+    code_ref[...] = jnp.dot(
+        code_list.astype(jnp.bfloat16), spread, preferred_element_type=jnp.float32
+    )
+    list_copy.wait()
+    pool_copy.wait()
+
+    def attend(other, ready):
+        code = code_ref[pl.ds(other, 1), :].astype(jnp.int32)
+        key_rows = []
+        value_rows = []
+        for k in range(capacity):
+            slot = jnp.clip(list_smem[other, k], 0, slots - 1)
+            key_rows.append(pool[slot, 0])
+            value_rows.append(pool[slot, 1])
+        page_keys = jnp.concatenate(key_rows, axis=0)
+        page_values = jnp.concatenate(value_rows, axis=0)
+        scores = (
+            lax.dot_general(
+                q_all[other],
+                page_keys,
+                (((1,), (1,)), ((), ())),
+                preferred_element_type=jnp.float32,
+            )
+            * scale
+        )
+        qi = lax.broadcasted_iota(jnp.int32, scores.shape, 0)
+        ki = lax.broadcasted_iota(jnp.int32, scores.shape, 1)
+        valid = (qi // heads == code // 32) & (ki % PAGE < code % 32)
+        scores = jnp.where(valid, scores, -1e30)
+        top = jnp.max(scores, axis=1, keepdims=True)
+        weights = jnp.where(valid, jnp.exp(scores - top), 0.0)
+        total = jnp.sum(weights, axis=1, keepdims=True)
+        mixed = jnp.dot(
+            weights.astype(jnp.bfloat16), page_values, preferred_element_type=jnp.float32
+        )
+        o_send[other] = mixed.astype(jnp.bfloat16)
+        ml_send[other] = as_rows(top, total)
+
+    def attend_peer(offset, carry):
+        peer, device = peer_of(offset)
+        remote(1, q_ref, q_all.at[peer], q_sem, peer, device, peer).wait_recv()
+        attend(peer, None)
+        remote(2, o_send.at[peer], o_all.at[me], o_sem, peer, device, me).start()
+        remote(3, ml_send.at[peer], ml_all.at[me], ml_sem, peer, device, me).start()
+        return carry
+
+    lax.fori_loop(1, owners, attend_peer, 0)
+    attend(me, None)
+    o_all[me] = o_send[me]
+    ml_all[me] = ml_send[me]
+
+    def wait_parts(offset, carry):
+        peer, device = peer_of(offset)
+        remote(2, o_send.at[peer], o_all.at[peer], o_sem, peer, device, peer).wait_recv()
+        remote(3, ml_send.at[peer], ml_all.at[peer], ml_sem, peer, device, peer).wait_recv()
+        return carry
+
+    lax.fori_loop(1, owners, wait_parts, 0)
+
+    tops = ml_all[:, 0, :]
+    totals = ml_all[:, 1, :]
+    top = jnp.maximum(jnp.max(tops, axis=0, keepdims=True), fresh_rows[0:1])
+    shares = jnp.exp(tops - top)
+    fresh_share = jnp.exp(fresh_rows[0:1] - top)
+    total = jnp.sum(shares * totals, axis=0, keepdims=True) + fresh_share * fresh_rows[1:2]
+    total = jnp.where(lane[0:1] < quer, total, 1.0)
+    shares = shares / total
+    fresh_share = fresh_share / total
+    every = jnp.concatenate(
+        [shares, fresh_share, jnp.zeros((128 - owners - 1, 128), jnp.float32)], axis=0
+    )
+    columns = jnp.transpose(every)
+    attn = fresh_out * columns[0:quer, owners : owners + 1]
+    for owner in range(owners):
+        attn = attn + o_all[owner].astype(jnp.float32) * columns[0:quer, owner : owner + 1]
+    attended = (resid_ref[...].astype(jnp.float32) + attn).astype(jnp.bfloat16)
+    att_ref[...] = attended
+    x_all[me] = attended
+
+    def send_rows(offset, carry):
+        peer, device = peer_of(offset)
+        remote(4, x_all.at[me], x_all.at[me], x_sem, peer, device, me).start()
+        return carry
+
+    lax.fori_loop(1, owners, send_rows, 0)
+
+    def wait_rows(offset, carry):
+        peer, device = peer_of(offset)
+        remote(4, x_all.at[peer], x_all.at[peer], x_sem, peer, device, peer).wait_recv()
+        return carry
+
+    lax.fori_loop(1, owners, wait_rows, 0)
+
+    each = rows * steps
+    tiles = depth // 128
+    for line in range(n_dp):
+        block = jnp.concatenate(
+            [
+                x_all[line * n_tensor + part].astype(jnp.float32).reshape(each, heads, 128)
+                for part in range(n_tensor)
+            ],
+            axis=1,
+        )
+        squares = jnp.sum(jnp.sum(block * block, axis=1, keepdims=True), axis=2, keepdims=True)
+        block = block * lax.rsqrt(squares / depth + 1e-05) * gain_ref[...][None]
+        y_ref[line * each : (line + 1) * each] = block
+    for tile in range(tiles):
+        x_ref[:, tile * 128 : (tile + 1) * 128] = y_ref[:, tile, :].astype(jnp.bfloat16)
+
+    def hidden_step(load, carry):
+        slot = load
+        for copy in gate_copies(load, slot):
+            copy.wait()
+        both = jnp.dot(x_ref[...], ring[slot], preferred_element_type=jnp.float32)
+        gate_act = both[:, :128]
+        value = gate_act / (1.0 + jnp.exp(-gate_act)) * both[:, 128:]
+        h_ref[:, pl.ds(pl.multiple_of(load * 128, 128), 128)] = value.astype(jnp.bfloat16)
+
+        @pl.when(load + ring_slots < loads)
+        def _():
+            for copy in down_copies(load + ring_slots - chunks, slot):
+                copy.start()
+
+        return carry
+
+    lax.fori_loop(0, chunks, hidden_step, 0)
+
+    pieces = 2
+    per_piece = down_loads // pieces
+    rows_piece = tiles // pieces
+
+    def piece_copy(piece, source, target, peer, device, index):
+        lines = pl.ds(piece * rows_piece, rows_piece)
+        return pltpu.make_async_remote_copy(
+            src_ref=p_send.at[source, lines],
+            dst_ref=p_all.at[target, lines],
+            send_sem=send_sem.at[5 + piece, peer],
+            recv_sem=p_sem.at[piece, index],
+            device_id=device,
+            device_id_type=pl.DeviceIdType.MESH,
+        )
+
+    for piece in range(pieces):
+        for step in range(per_piece):
+            load = piece * per_piece + step
+            slot = (chunks + load) % ring_slots
+            for copy in down_copies(load, slot):
+                copy.wait()
+            for q in range(4):
+                both = jnp.dot(
+                    h_ref[...],
+                    ring[slot, q * wide : (q + 1) * wide, :],
+                    preferred_element_type=jnp.float32,
+                )
+                tile = load * 8 + 2 * q
+                part_ref[:, tile, :] = both[:, :128]
+                part_ref[:, tile + 1, :] = both[:, 128:]
+
+        lines = slice(piece * rows_piece, (piece + 1) * rows_piece)
+        for owner in range(owners):
+            p_send[owner, lines] = part_ref[owner, lines].astype(jnp.bfloat16)
+
+        def send_piece(offset, carry):
+            peer, device = peer_of(offset)
+            piece_copy(piece, peer, me, peer, device, me).start()
+            return carry
+
+        lax.fori_loop(1, owners, send_piece, 0)
+
+    for piece in range(pieces):
+        lines = slice(piece * rows_piece, (piece + 1) * rows_piece)
+
+        def wait_piece(offset, carry):
+            peer, device = peer_of(offset)
+            piece_copy(piece, peer, peer, peer, device, peer).wait_recv()
+            return carry
+
+        lax.fori_loop(1, owners, wait_piece, 0)
+        p_all[me, lines] = p_send[me, lines]
+        summed = p_all[0, lines].astype(jnp.float32)
+        for owner in range(1, owners):
+            summed = summed + p_all[owner, lines].astype(jnp.float32)
+        out_ref[lines] = summed.astype(jnp.bfloat16)
+
+    def drain(offset, carry):
+        peer, device = peer_of(offset)
+        remote(0, meta_ref, meta_all.at[me], meta_sem, peer, device, me).wait_send()
+        remote(1, q_ref, q_all.at[me], q_sem, peer, device, me).wait_send()
+        remote(2, o_send.at[peer], o_all.at[me], o_sem, peer, device, me).wait_send()
+        remote(3, ml_send.at[peer], ml_all.at[me], ml_sem, peer, device, me).wait_send()
+        remote(4, x_all.at[me], x_all.at[me], x_sem, peer, device, me).wait_send()
+        for piece in range(pieces):
+            piece_copy(piece, peer, me, peer, device, me).wait_send()
+        return carry
+
+    lax.fori_loop(1, owners, drain, 0)
+
+
+RING_SLOTS = 14
+
+
+def fused_shards(
+    resid,
+    queries,
+    new_kv,
+    tail_fill,
+    page_ids,
+    kv_pool,
+    norm_gain,
+    gate_weight,
+    up_weight,
+    down_weight,
+):
+    n_dp = lax.axis_size("dp")
+    n_tensor = lax.axis_size("tensor")
+    owners = n_dp * n_tensor
+    rows, steps, heads, head = queries.shape
+    sel = page_ids.shape[-1]
+    slots = kv_pool.shape[0]
+    depth, wide = gate_weight.shape
+    quer = rows * steps * heads
+    tiles = depth // 128
+    page_at = jnp.arange(sel, dtype=jnp.int32)
+    held = jnp.where(page_at[None, None, :] == 0, tail_fill[:, :, None], PAGE)
+    reader = jnp.arange(rows * steps, dtype=jnp.int32).reshape(rows, steps, 1)
+    meta = jnp.stack([page_ids.reshape(-1), (held + 32 * reader).reshape(-1)])
+    meta = jnp.pad(meta, ((0, 6), (0, 0)))
+    fresh = new_kv[:, :, 0].reshape(rows * (steps + 1), 2, head)
+    fresh = jnp.pad(fresh, ((0, 16 - fresh.shape[0]), (0, 0), (0, 0)))
+    capacity = max(2, (2 * rows * steps * sel + owners - 1) // owners)
+    dims = (n_dp, n_tensor, slots, wide, depth, RING_SLOTS, rows, steps, heads, sel)
+    bf16, f32, i32 = jnp.bfloat16, jnp.float32, jnp.int32
+    vmem = pl.BlockSpec(memory_space=pltpu.VMEM)
+    hbm = pl.BlockSpec(memory_space=pl.ANY)
+    dma = pltpu.SemaphoreType.DMA
+    attended, ffn_out = pl.pallas_call(
+        functools.partial(fused_kernel, dims),
+        out_shape=(
+            jax.ShapeDtypeStruct((quer, head), bf16),
+            jax.ShapeDtypeStruct((tiles, 128), bf16),
+        ),
+        in_specs=[vmem] * 6 + [hbm] * 4,
+        out_specs=(vmem, vmem),
+        scratch_shapes=[
+            pltpu.VMEM((RING_SLOTS, depth, 256), bf16),
+            pltpu.VMEM(kv_pool.shape, bf16),
+            pltpu.VMEM((owners, 8, 128), i32),
+            pltpu.VMEM((owners, quer, head), bf16),
+            pltpu.VMEM((owners, quer, head), bf16),
+            pltpu.VMEM((owners, quer, head), bf16),
+            pltpu.VMEM((owners, 8, 128), f32),
+            pltpu.VMEM((owners, 8, 128), f32),
+            pltpu.VMEM((owners, quer, head), bf16),
+            pltpu.VMEM((owners, 128), i32),
+            pltpu.SMEM((owners, 128), i32),
+            pltpu.VMEM((owners, capacity * PAGE), f32),
+            pltpu.VMEM((owners, tiles, 128), f32),
+            pltpu.VMEM((owners, depth), bf16),
+            pltpu.VMEM((owners, wide), bf16),
+            pltpu.VMEM((owners, tiles, 128), f32),
+            pltpu.VMEM((owners, tiles, 128), bf16),
+            pltpu.VMEM((owners, tiles, 128), bf16),
+            dma(()),
+            dma(()),
+            dma((RING_SLOTS, 4)),
+            dma((7, owners)),
+            dma((owners,)),
+            dma((owners,)),
+            dma((owners,)),
+            dma((owners,)),
+            dma((owners,)),
+            dma((2, owners)),
+        ],
+        compiler_params=pltpu.CompilerParams(
+            collective_id=0, has_side_effects=True, vmem_limit_bytes=VMEM_LIMIT
+        ),
+        name="attend_ffn",
+    )(
+        queries.reshape(quer, head),
+        meta,
+        fresh[:, 0],
+        fresh[:, 1],
+        resid.reshape(quer, head),
+        norm_gain.reshape(tiles, 128),
+        kv_pool,
+        gate_weight,
+        up_weight,
+        down_weight,
+    )
+    return attended.reshape(resid.shape), ffn_out.reshape(1, depth)
+
+
+VMEM_LIMIT = 65 * 1000 * 1000
+
+
 def solution(mesh):
-    return jax.shard_map(
-        shards,
-        mesh=mesh,
-        in_specs=(
-            P(("grp", "dp"), None, "tensor"),
-            P(("grp", "dp"), None, "tensor", None),
-            P(("grp", "dp"), None, "tensor", None, None),
-            P(("grp", "dp"), None),
-            P(("grp", "dp"), None, "tensor", None),
-            P(("grp", "dp", "tensor"), None, None, None),
-            P(),
-            P(None, ("dp", "tensor")),
-            P(None, ("dp", "tensor")),
-            P(("dp", "tensor"), None),
-        ),
-        out_specs=(P(("grp", "dp"), None, "tensor"), P(("grp", "dp", "tensor"), None)),
-        check_vma=False,
-    )
+    in_specs = (
+        P(("grp", "dp"), None, "tensor"),
+        P(("grp", "dp"), None, "tensor", None),
+        P(("grp", "dp"), None, "tensor", None, None),
+        P(("grp", "dp"), None),
+        P(("grp", "dp"), None, "tensor", None),
+        P(("grp", "dp", "tensor"), None, None, None),
+        P(),
+        P(None, ("dp", "tensor")),
+        P(None, ("dp", "tensor")),
+        P(("dp", "tensor"), None),
+    )
+    out_specs = (P(("grp", "dp"), None, "tensor"), P(("grp", "dp", "tensor"), None))
+
+    def whole(*arrays):
+        fused = fits_fused(mesh, arrays[0], arrays[1], arrays[4], arrays[5], arrays[7])
+        return jax.shard_map(
+            fused_shards if fused else shards,
+            mesh=mesh,
+            in_specs=in_specs,
+            out_specs=out_specs,
+            check_vma=False,
+        )(*arrays)
+
+    return whole

time: 192 us -> 65.9 us (0.34)
  blocking collectives: 103 us -> 0 us
  Pallas kernels: 0 us -> 56 us
  waiting for transfers between devices: 37.4 us -> 0 us
  matrix products: 32.8 us -> 0 us
  starting transfers between devices: 3.72 us -> 0 us
  other arithmetic: 5.53 us -> 2.12 us
  local copies, waits for them, and re-layouts: 8.6 us -> 6.6 us
    unnamed x1 -> x0, blocking collectives: 63.2 us -> none
    pallas_call x0 -> x1, Pallas kernels: none -> 56 us  [fused_shards(): pl.pallas_call(functools.partial(fused_kernel, dims), out_shape=(jax.Shap...]
    all_to_all x1 -> x0, waiting for transfers between devices: 37.4 us -> none  [shards(): lax.all_to_all(kv_pool[lax.all_to_all(request_buffer, ('dp', 'tensor'), s...]
    dot_general x6 -> x0, matrix products: 32.8 us -> none  [the longest x1 19.7 us: shards(): jnp.dot(hidden_flat, down_weight, preferred_element_type=jnp.float32)]
    all_gather x2 -> x0, blocking collectives: 26.2 us -> none  [the longest x1 18.8 us: shards(): block_rows = lax.all_gather(normed, 'dp', axis=0, tiled=True)]
    all_to_all x1 -> x0, blocking collectives: 13.6 us -> none  [shards(): lax.all_to_all(request_buffer, ('dp', 'tensor'), split_axis=0, concat_axi...]
    all_to_all x1 -> x0, starting transfers between devices: 3.72 us -> none  [shards(): lax.all_to_all(kv_pool[lax.all_to_all(request_buffer, ('dp', 'tensor'), s...]
    gather x2 -> x0, local copies, waits for them, and re-layouts: 2.97 us -> none  [the longest x1 2.21 us: shards(): kv_pool[lax.all_to_all(request_buffer, ('dp', 'tensor'), split_axis=0, co...]
  transfers between devices with their start and end apart: 1 -> 0, of which waited for: 1 -> 0; matrix products, arithmetic and copies ran while one was open for 2% -> 0% of each run, Pallas kernels for 0% -> 0%
where the time goes in v1:
time: 65.9 us; the launch traced here: 65.4 us
  Pallas kernels  56 us (85%)
  local copies, waits for them, and re-layouts  6.6 us (10%)
  other arithmetic  2.12 us (3%)
    pallas_call x1, Pallas kernels, fused_shards(): pl.pallas_call(functools.partial(fused_kernel, dims), out_shape=(jax.Shap...  56 us
    unnamed x2, local copies, waits for them, and re-layouts  1.87 us
    unnamed x1, other arithmetic  1.34 us
    reshape x1, local copies, waits for them, and re-layouts, fused_shards(): resid.reshape(quer, head)  1.34 us
    reshape x1, local copies, waits for them, and re-layouts, fused_shards(): return (attended.reshape(resid.shape), ffn_out.reshape(1, depth))  1.33 us

profile of v1, /device:TPU:0, one launch (start us, length us, event | category | flops | bytes accessed | tf_op | source)
XLA Modules:
  0.0 65.4 jit_solution(16850192830496459482)
XLA Ops:
  0.7 0.8 %select_add_fusion = s32[2,2,32]{2,1,0:T(2,128)S(1)} fusion(pred[32]{0:T(512)(128)(4,1)S(1)} %iota_compare_fusion, s32[2,2]{1,0:T(2,128)S(1)} %add_multiply_fusion, s32[2,2]{1,0:T(2,128)} %param.13), kind=kLoop, calls=%fused_computation.5 | loop fusion | flops 256 | bytes 576 | tf_op jit(solution)/shard_map/add | solution.py:554
  1.4 0.1 add.30
  1.5 0.5 broadcast.44
  2.0 1.3 %reduce.3 = s32[2,2,32]{2,1,0:T(2,128)S(1)} reduce(s32[2,2,1,32]{3,2,1,0:T(1,128)} %param.14, s32[]{:T(128)} %broadcast.44), dimensions={2}, to_apply=%param.14.reduce_sub_computation.3 | reduce | bytes 1028 | tf_op args[4]
  3.4 0.1 stack_reshape.4
  3.4 0.6 pad.8.meta_ref
  4.0 0.7 %copy.13 = bf16[6,2,128]{2,0,1:T(8,128)(2,1)S(1)} copy(bf16[6,2,128]{2,1,0:T(2,128)(2,1)} %bitcast.16) | data formatting | bytes 6144 | tf_op jit(solution)/shard_map/reshape;squeeze | solution.py:556
  4.7 0.6 fusion.1
  5.3 1.3 %reshape.84.resid_ref = bf16[64,128]{1,0:T(8,128)(2,1)} reshape(bf16[2,2,2048]{2,1,0:T(2,128)(2,1)} %param.10) | data formatting | bytes 32768 | tf_op jit(solution)/shard_map/reshape | solution.py:611
  6.7 56.0 %attend_ffn.1 = (bf16[64,128]{1,0:T(8,128)(2,1)}, bf16[64,128]{1,0:T(8,128)(2,1)}) custom-call(bf16[64,128]{1,0:T(8,128)(2,1)} %bitcast.14, s32[8,128]{1,0:T(8,128)} %pad.8.meta_ref, bf16[16,128]{1,0:T(8,128)(2,1)} %get-tuple-element.7.fresh_k_ref, bf16[16,128]{1,0:T(8,128)(2,1)} %get-tuple-element.6.fresh_v_ref, bf16[64,128]{1,0:T(8,128)(2,1)} %reshape.84.resid_ref, ...), custom_call_target="tpu_custom_call" | custom-call | tf_op jit(solution)/shard_map/attend_ffn/pallas_call | solution.py:564
  62.7 1.3 %reshape.86 = bf16[2,2,2048]{2,1,0:T(2,128)(2,1)} reshape(bf16[64,128]{1,0:T(8,128)(2,1)} %get-tuple-element.4) | data formatting | bytes 32768 | tf_op jit(solution)/shard_map/reshape | solution.py:618
  64.0 1.4 %copy.16 = bf16[1,1,64,128]{3,1,2,0:T(2,128)(2,1)} copy(bf16[1,1,64,128]{3,2,1,0:T(8,128)(2,1)} %bitcast.15) | data formatting | bytes 32768
  (3 shorter events, 0.0 us)

commit v2 on v1

--- a/solution.py
+++ b/solution.py
@@ -124,6 +124,7 @@
     wide = gate_weight.shape[1] // owners
     return (
         owners == 16
+        and mesh.shape["tensor"] == 4
         and rows * steps * mesh.shape["dp"] == owners
         and (queries.shape[2] // mesh.shape["tensor"]) % 8 == 0
         and rows * steps * (queries.shape[2] // mesh.shape["tensor"]) == 64
@@ -138,9 +139,9 @@
 def fused_kernel(
     dims,
     q_ref,
-    meta_ref,
-    fresh_k_ref,
-    fresh_v_ref,
+    ids_ref,
+    fill_ref,
+    new_ref,
     resid_ref,
     gain_ref,
     pool_hbm,
@@ -165,8 +166,12 @@
     x_ref,
     h_ref,
     part_ref,
-    p_send,
-    p_all,
+    core_send,
+    core_got,
+    x_send,
+    x_got,
+    z_send,
+    z_got,
     pool_sem,
     list_sem,
     ring_sem,
@@ -176,6 +181,7 @@
     o_sem,
     ml_sem,
     x_sem,
+    p_send_sem,
     p_sem,
 ):
     n_dp, n_tensor, slots, wide, depth, ring_slots, rows, steps, heads, sel = dims
@@ -248,21 +254,98 @@
 
     pl.semaphore_wait(barrier, owners - 1)
 
-    def send_queries(offset, carry):
-        peer, device = peer_of(offset)
-        remote(0, meta_ref, meta_all.at[me], meta_sem, peer, device, me).start()
-        remote(1, q_ref, q_all.at[me], q_sem, peer, device, me).start()
-        return carry
-
-    lax.fori_loop(1, owners, send_queries, 0)
-    meta_all[me] = meta_ref[...]
+    meta_all[me] = jnp.zeros((8, 128), jnp.int32)
+    page_lane = lax.broadcasted_iota(jnp.int32, (1, 128), 1)
+    held = PAGE + 32 * (page_lane // sel)
+    for row in range(rows):
+        for step in range(steps):
+            at = (row * steps + step) * sel
+            meta_all[me, 0:1, at : at + sel] = ids_ref[row, step]
+            held = jnp.where(page_lane == at, fill_ref[row, step] + 32 * (at // sel), held)
+    meta_all[me, 1:2, :] = held
     q_all[me] = q_ref[...]
 
+    core_peer = tensor + 1 - 2 * lax.rem(tensor, 2)
+    x_peer = lax.rem(tensor + 2, 4)
+
+    def forward(kind, buffer, sems, block, device, index):
+        return pltpu.make_async_remote_copy(
+            src_ref=buffer.at[block],
+            dst_ref=buffer.at[block],
+            send_sem=send_sem.at[kind, index],
+            recv_sem=sems.at[block],
+            device_id=device,
+            device_id_type=pl.DeviceIdType.MESH,
+        )
+
+    to_core = {"dp": dp, "tensor": core_peer}
+    to_x = {"dp": dp, "tensor": x_peer}
+
+    def spread_out(sets):
+        def line_of(offset):
+            line = lax.rem(dp + offset, n_dp)
+            return line, line * n_tensor
+
+        for offset in range(1, n_dp):
+            line, _ = line_of(offset)
+            for kind, buffer, sems in sets:
+                forward(
+                    kind, buffer, sems, me, {"dp": line, "tensor": tensor}, offset - 1
+                ).start()
+        for offset in range(n_dp):
+            _, base = line_of(offset)
+            for kind, buffer, sems in sets:
+                if offset:
+                    forward(kind, buffer, sems, base + tensor, to_x, 3 + offset).wait_recv()
+                forward(kind, buffer, sems, base + tensor, to_x, 3 + offset).start()
+                forward(kind, buffer, sems, base + tensor, to_core, 7 + offset).start()
+        for offset in range(n_dp):
+            _, base = line_of(offset)
+            for kind, buffer, sems in sets:
+                forward(kind, buffer, sems, base + x_peer, to_core, 11 + offset).wait_recv()
+                forward(kind, buffer, sems, base + x_peer, to_core, 11 + offset).start()
+
+    def gathered(sets):
+        for offset in range(n_dp):
+            base = lax.rem(dp + offset, n_dp) * n_tensor
+            for kind, buffer, sems in sets:
+                forward(kind, buffer, sems, base + core_peer, to_core, 7 + offset).wait_recv()
+                far = lax.rem(core_peer + 2, 4)
+                forward(kind, buffer, sems, base + far, to_core, 11 + offset).wait_recv()
+
+    def drained(sets):
+        for index in range(15):
+            for kind, buffer, sems in sets:
+                forward(kind, buffer, sems, me, to_core, index).wait_send()
+
+    first = ((0, meta_all, meta_sem), (1, q_all, q_sem))
+    spread_out(first)
+
     scale = 1.0 / math.sqrt(q_ref.shape[-1])
+    fresh_rows = [
+        new_ref[row, token, 0].astype(jnp.float32)
+        for row in range(rows)
+        for token in range(steps + 1)
+    ]
+    blank = jnp.zeros((16 - len(fresh_rows), 128), jnp.float32)
+    fresh_k = jnp.concatenate([pair[0:1] for pair in fresh_rows] + [blank], axis=0)
+    fresh_v = jnp.concatenate([pair[1:2] for pair in fresh_rows] + [blank], axis=0)
+    fresh_k = fresh_k.astype(jnp.bfloat16)
+    fresh_v = fresh_v.astype(jnp.bfloat16)
+    resid_rows = [resid_ref[row].astype(jnp.float32) for row in range(rows)]
+    resid = jnp.concatenate(
+        [
+            resid_rows[row][step : step + 1, head * 128 : (head + 1) * 128]
+            for row in range(rows)
+            for step in range(steps)
+            for head in range(heads)
+        ],
+        axis=0,
+    )
     fresh_scores = (
         lax.dot_general(
             q_ref[...],
-            fresh_k_ref[...],
+            fresh_k,
             (((1,), (1,)), ((), ())),
             preferred_element_type=jnp.float32,
         )
@@ -279,7 +362,7 @@
     fresh_exp = jnp.where(fresh_ok, jnp.exp(fresh_scores - fresh_top), 0.0)
     fresh_total = jnp.sum(fresh_exp, axis=1, keepdims=True)
     fresh_out = jnp.dot(
-        fresh_exp.astype(jnp.bfloat16), fresh_v_ref[...], preferred_element_type=jnp.float32
+        fresh_exp.astype(jnp.bfloat16), fresh_v, preferred_element_type=jnp.float32
     )
 
     def as_rows(first, second):
@@ -290,12 +373,7 @@
 
     fresh_rows = as_rows(fresh_top, fresh_total)
 
-    def wait_meta(offset, carry):
-        peer, device = peer_of(offset)
-        remote(0, meta_ref, meta_all.at[peer], meta_sem, peer, device, peer).wait_recv()
-        return carry
-
-    lax.fori_loop(1, owners, wait_meta, 0)
+    gathered(first)
 
     ids = meta_all[:, 0, :]
     extra = meta_all[:, 1, :]
@@ -366,7 +444,6 @@
 
     def attend_peer(offset, carry):
         peer, device = peer_of(offset)
-        remote(1, q_ref, q_all.at[peer], q_sem, peer, device, peer).wait_recv()
         attend(peer, None)
         remote(2, o_send.at[peer], o_all.at[me], o_sem, peer, device, me).start()
         remote(3, ml_send.at[peer], ml_all.at[me], ml_sem, peer, device, me).start()
@@ -401,23 +478,21 @@
     attn = fresh_out * columns[0:quer, owners : owners + 1]
     for owner in range(owners):
         attn = attn + o_all[owner].astype(jnp.float32) * columns[0:quer, owner : owner + 1]
-    attended = (resid_ref[...].astype(jnp.float32) + attn).astype(jnp.bfloat16)
-    att_ref[...] = attended
+    attended = (resid + attn).astype(jnp.bfloat16)
     x_all[me] = attended
 
-    def send_rows(offset, carry):
-        peer, device = peer_of(offset)
-        remote(4, x_all.at[me], x_all.at[me], x_sem, peer, device, me).start()
-        return carry
-
-    lax.fori_loop(1, owners, send_rows, 0)
-
-    def wait_rows(offset, carry):
-        peer, device = peer_of(offset)
-        remote(4, x_all.at[peer], x_all.at[peer], x_sem, peer, device, peer).wait_recv()
-        return carry
-
-    lax.fori_loop(1, owners, wait_rows, 0)
+    last = ((4, x_all, x_sem),)
+    spread_out(last)
+    rounded = attended.astype(jnp.float32)
+    for row in range(rows):
+        for head in range(heads):
+            pair = [
+                rounded[(row * steps + step) * heads + head :][0:1] for step in range(steps)
+            ]
+            att_ref[row, :, head * 128 : (head + 1) * 128] = jnp.concatenate(
+                pair, axis=0
+            ).astype(jnp.bfloat16)
+    gathered(last)
 
     each = rows * steps
     tiles = depth // 128
@@ -457,15 +532,35 @@
     per_piece = down_loads // pieces
     rows_piece = tiles // pieces
 
-    def piece_copy(piece, source, target, peer, device, index):
-        lines = pl.ds(piece * rows_piece, rows_piece)
+    core = lax.rem(tensor, 2)
+    column = tensor // 2
+
+    def piece_copy(piece, stage, source, target, device, index):
         return pltpu.make_async_remote_copy(
-            src_ref=p_send.at[source, lines],
-            dst_ref=p_all.at[target, lines],
-            send_sem=send_sem.at[5 + piece, peer],
-            recv_sem=p_sem.at[piece, index],
+            src_ref=source,
+            dst_ref=target,
+            send_sem=p_send_sem.at[piece, stage, index],
+            recv_sem=p_sem.at[piece, stage, index],
             device_id=device,
             device_id_type=pl.DeviceIdType.MESH,
+        )
+
+    def core_copy(piece):
+        return piece_copy(piece, 0, core_send.at[piece], core_got.at[piece], to_core, 0)
+
+    def x_copy(piece):
+        return piece_copy(piece, 1, x_send.at[piece], x_got.at[piece], to_x, 0)
+
+    def z_copy(piece, offset):
+        line = lax.rem(dp + offset, n_dp)
+        device = {"dp": line, "tensor": tensor}
+        return piece_copy(
+            piece,
+            2,
+            z_send.at[piece, offset],
+            z_got.at[piece, offset],
+            device,
+            offset,
         )
 
     for piece in range(pieces):
@@ -483,42 +578,59 @@
                 tile = load * 8 + 2 * q
                 part_ref[:, tile, :] = both[:, :128]
                 part_ref[:, tile + 1, :] = both[:, 128:]
-
         lines = slice(piece * rows_piece, (piece + 1) * rows_piece)
-        for owner in range(owners):
-            p_send[owner, lines] = part_ref[owner, lines].astype(jnp.bfloat16)
-
-        def send_piece(offset, carry):
-            peer, device = peer_of(offset)
-            piece_copy(piece, peer, me, peer, device, me).start()
-            return carry
-
-        lax.fori_loop(1, owners, send_piece, 0)
+        for side in range(2):
+            for line in range(n_dp):
+                owner = line * n_tensor + side * 2 + 1 - core
+                core_send[piece, side * n_dp + line] = part_ref[owner, lines].astype(jnp.bfloat16)
+        core_copy(piece).start()
 
     for piece in range(pieces):
         lines = slice(piece * rows_piece, (piece + 1) * rows_piece)
-
-        def wait_piece(offset, carry):
-            peer, device = peer_of(offset)
-            piece_copy(piece, peer, peer, peer, device, peer).wait_recv()
-            return carry
-
-        lax.fori_loop(1, owners, wait_piece, 0)
-        p_all[me, lines] = p_send[me, lines]
-        summed = p_all[0, lines].astype(jnp.float32)
-        for owner in range(1, owners):
-            summed = summed + p_all[owner, lines].astype(jnp.float32)
-        out_ref[lines] = summed.astype(jnp.bfloat16)
+        core_copy(piece).wait_recv()
+        for line in range(n_dp):
+            away = 1 - column
+            far = part_ref[line * n_tensor + away * 2 + core, lines]
+            far = far + core_got[piece, away * n_dp + line].astype(jnp.float32)
+            x_send[piece, line] = far.astype(jnp.bfloat16)
+        x_copy(piece).start()
+
+    for piece in range(pieces):
+        lines = slice(piece * rows_piece, (piece + 1) * rows_piece)
+        x_copy(piece).wait_recv()
+        for offset in range(n_dp):
+            line = lax.rem(dp + offset, n_dp)
+            near = part_ref[line * n_tensor + tensor, lines]
+            near = near + core_got[piece, column * n_dp + line].astype(jnp.float32)
+            near = near + x_got[piece, line].astype(jnp.float32)
+            if offset:
+                z_send[piece, offset] = near.astype(jnp.bfloat16)
+                z_copy(piece, offset).start()
+            else:
+                part_ref[me, lines] = near
+
+    for piece in range(pieces):
+        lines = slice(piece * rows_piece, (piece + 1) * rows_piece)
+        summed = part_ref[me, lines]
+        for offset in range(1, n_dp):
+            z_copy(piece, offset).wait_recv()
+            summed = summed + z_got[piece, offset].astype(jnp.float32)
+        for tile in range(rows_piece):
+            at = (piece * rows_piece + tile) * 128
+            out_ref[:, at : at + 128] = summed[tile : tile + 1].astype(jnp.bfloat16)
+
+    drained(first)
+    drained(last)
+    for piece in range(pieces):
+        core_copy(piece).wait_send()
+        x_copy(piece).wait_send()
+        for offset in range(1, n_dp):
+            z_copy(piece, offset).wait_send()
 
     def drain(offset, carry):
         peer, device = peer_of(offset)
-        remote(0, meta_ref, meta_all.at[me], meta_sem, peer, device, me).wait_send()
-        remote(1, q_ref, q_all.at[me], q_sem, peer, device, me).wait_send()
         remote(2, o_send.at[peer], o_all.at[me], o_sem, peer, device, me).wait_send()
         remote(3, ml_send.at[peer], ml_all.at[me], ml_sem, peer, device, me).wait_send()
-        remote(4, x_all.at[me], x_all.at[me], x_sem, peer, device, me).wait_send()
-        for piece in range(pieces):
-            piece_copy(piece, peer, me, peer, device, me).wait_send()
         return carry
 
     lax.fori_loop(1, owners, drain, 0)
@@ -548,13 +660,6 @@
     depth, wide = gate_weight.shape
     quer = rows * steps * heads
     tiles = depth // 128
-    page_at = jnp.arange(sel, dtype=jnp.int32)
-    held = jnp.where(page_at[None, None, :] == 0, tail_fill[:, :, None], PAGE)
-    reader = jnp.arange(rows * steps, dtype=jnp.int32).reshape(rows, steps, 1)
-    meta = jnp.stack([page_ids.reshape(-1), (held + 32 * reader).reshape(-1)])
-    meta = jnp.pad(meta, ((0, 6), (0, 0)))
-    fresh = new_kv[:, :, 0].reshape(rows * (steps + 1), 2, head)
-    fresh = jnp.pad(fresh, ((0, 16 - fresh.shape[0]), (0, 0), (0, 0)))
     capacity = max(2, (2 * rows * steps * sel + owners - 1) // owners)
     dims = (n_dp, n_tensor, slots, wide, depth, RING_SLOTS, rows, steps, heads, sel)
     bf16, f32, i32 = jnp.bfloat16, jnp.float32, jnp.int32
@@ -564,10 +669,10 @@
     attended, ffn_out = pl.pallas_call(
         functools.partial(fused_kernel, dims),
         out_shape=(
-            jax.ShapeDtypeStruct((quer, head), bf16),
-            jax.ShapeDtypeStruct((tiles, 128), bf16),
+            jax.ShapeDtypeStruct(resid.shape, bf16),
+            jax.ShapeDtypeStruct((1, depth), bf16),
         ),
-        in_specs=[vmem] * 6 + [hbm] * 4,
+        in_specs=[vmem, vmem, pl.BlockSpec(memory_space=pltpu.SMEM)] + [vmem] * 3 + [hbm] * 4,
         out_specs=(vmem, vmem),
         scratch_shapes=[
             pltpu.VMEM((RING_SLOTS, depth, 256), bf16),
@@ -586,18 +691,23 @@
             pltpu.VMEM((owners, depth), bf16),
             pltpu.VMEM((owners, wide), bf16),
             pltpu.VMEM((owners, tiles, 128), f32),
-            pltpu.VMEM((owners, tiles, 128), bf16),
-            pltpu.VMEM((owners, tiles, 128), bf16),
+            pltpu.VMEM((2, 8, tiles // 2, 128), bf16),
+            pltpu.VMEM((2, 8, tiles // 2, 128), bf16),
+            pltpu.VMEM((2, n_dp, tiles // 2, 128), bf16),
+            pltpu.VMEM((2, n_dp, tiles // 2, 128), bf16),
+            pltpu.VMEM((2, n_dp, tiles // 2, 128), bf16),
+            pltpu.VMEM((2, n_dp, tiles // 2, 128), bf16),
             dma(()),
             dma(()),
             dma((RING_SLOTS, 4)),
-            dma((7, owners)),
+            dma((5, owners)),
             dma((owners,)),
             dma((owners,)),
             dma((owners,)),
             dma((owners,)),
             dma((owners,)),
-            dma((2, owners)),
+            dma((2, 3, n_dp)),
+            dma((2, 3, n_dp)),
         ],
         compiler_params=pltpu.CompilerParams(
             collective_id=0, has_side_effects=True, vmem_limit_bytes=VMEM_LIMIT
@@ -605,17 +715,17 @@
         name="attend_ffn",
     )(
         queries.reshape(quer, head),
-        meta,
-        fresh[:, 0],
-        fresh[:, 1],
-        resid.reshape(quer, head),
+        page_ids,
+        tail_fill,
+        new_kv,
+        resid,
         norm_gain.reshape(tiles, 128),
         kv_pool,
         gate_weight,
         up_weight,
         down_weight,
     )
-    return attended.reshape(resid.shape), ffn_out.reshape(1, depth)
+    return attended, ffn_out
 
 
 VMEM_LIMIT = 65 * 1000 * 1000

time: 65.9 us -> 61.8 us (0.938)
  local copies, waits for them, and re-layouts: 6.6 us -> 2.74 us
  other arithmetic: 2.12 us -> 0 us
  Pallas kernels: 56 us -> 58.1 us
    reshape x2 -> x0, local copies, waits for them, and re-layouts: 2.67 us -> none  [the longest x1 1.34 us: fused_shards(): resid.reshape(quer, head)]
    pallas_call x1, Pallas kernels: 56 us -> 58.1 us  [fused_shards(): pl.pallas_call(functools.partial(fused_kernel, dims), out_shape=(jax.Shap...]
    unnamed x1 -> x0, other arithmetic: 1.34 us -> none
    unnamed x2, local copies, waits for them, and re-layouts: 1.87 us -> 2.74 us
    another operation x2 -> x0, local copies, waits for them, and re-layouts: 0.77 us -> none  [the longest x1 0.69 us: fused_shards(): fresh = new_kv[:, :, 0].reshape(rows * (steps + 1), 2, head)]
    add x1 -> x0, other arithmetic: 0.75 us -> none  [fused_shards(): meta = jnp.stack([page_ids.reshape(-1), (held + 32 * reader).reshape(-1)])]
where the time goes in v2:
time: 61.8 us; the launch traced here: 61.5 us
  Pallas kernels  58.1 us (94%)
  local copies, waits for them, and re-layouts  2.74 us (4%)
  between operations  0.64 us (1%)
    pallas_call x1, Pallas kernels, fused_shards(): pl.pallas_call(functools.partial(fused_kernel, dims), out_shape=(jax.Shap...  58.1 us
    unnamed x2, local copies, waits for them, and re-layouts  2.74 us

profile of v2, /device:TPU:0, one launch (start us, length us, event | category | flops | bytes accessed | tf_op | source)
XLA Modules:
  0.0 61.5 jit_solution(11167050600100451167)
XLA Ops:
  0.6 58.1 %attend_ffn.1 = (bf16[2,2,2048]{2,1,0:T(2,128)(2,1)}, bf16[1,8192]{1,0:T(2,128)(2,1)}) custom-call(bf16[64,128]{1,0:T(8,128)(2,1)} %bitcast.3, s32[2,2,1,32]{3,2,1,0:T(1,128)} %ids_ref.1, s32[2,2]{1,0:T(2,128)} %fill_ref.1, bf16[2,3,1,2,128]{4,3,2,1,0:T(2,128)(2,1)} %new_ref.1, bf16[2,2,2048]{2,1,0:T(2,128)(2,1)} %resid_ref.1, f32[64,128]{1,0:T(8,128)} %bitcast.2, ...), custom_call_target="tpu_custom_call" | custom-call | tf_op jit(solution)/shard_map/attend_ffn/pallas_call | solution.py:669
  58.8 1.3 %copy.14 = bf16[2,2,2048]{2,1,0:T(2,128)(2,1)} copy(bf16[2,2,2048]{2,1,0:T(2,128)(2,1)} %get-tuple-element.4) | data formatting | bytes 32768
  60.1 1.4 %copy.15 = bf16[1,8192]{1,0:T(2,128)(2,1)} copy(bf16[1,8192]{1,0:T(2,128)(2,1)} %get-tuple-element.5) | data formatting | bytes 32768

commit v3 on v2

--- a/solution.py
+++ b/solution.py
@@ -254,7 +254,6 @@
 
     pl.semaphore_wait(barrier, owners - 1)
 
-    meta_all[me] = jnp.zeros((8, 128), jnp.int32)
     page_lane = lax.broadcasted_iota(jnp.int32, (1, 128), 1)
     held = PAGE + 32 * (page_lane // sel)
     for row in range(rows):
@@ -369,7 +368,7 @@
         lane = lax.broadcasted_iota(jnp.int32, (quer, 128), 1)
         both = jnp.where(lane == 0, first, jnp.where(lane == 1, second, 0.0))
         both = jnp.concatenate([both, jnp.zeros((128 - quer, 128), jnp.float32)], axis=0)
-        return jnp.transpose(both)[0:8]
+        return jnp.transpose(both)[0:2]
 
     fresh_rows = as_rows(fresh_top, fresh_total)
 
@@ -677,12 +676,12 @@
         scratch_shapes=[
             pltpu.VMEM((RING_SLOTS, depth, 256), bf16),
             pltpu.VMEM(kv_pool.shape, bf16),
-            pltpu.VMEM((owners, 8, 128), i32),
+            pltpu.VMEM((owners, 2, 128), i32),
             pltpu.VMEM((owners, quer, head), bf16),
             pltpu.VMEM((owners, quer, head), bf16),
             pltpu.VMEM((owners, quer, head), bf16),
-            pltpu.VMEM((owners, 8, 128), f32),
-            pltpu.VMEM((owners, 8, 128), f32),
+            pltpu.VMEM((owners, 2, 128), f32),
+            pltpu.VMEM((owners, 2, 128), f32),
             pltpu.VMEM((owners, quer, head), bf16),
             pltpu.VMEM((owners, 128), i32),
             pltpu.SMEM((owners, 128), i32),

time: 61.8 us -> 61 us (0.987)
  Pallas kernels: 58.1 us -> 57.3 us
    pallas_call x1, Pallas kernels: 58.1 us -> 57.3 us  [fused_shards(): pl.pallas_call(functools.partial(fused_kernel, dims), out_shape=(jax.Shap...]
where the time goes in v3:
time: 61 us; the launch traced here: 60.7 us
  Pallas kernels  57.3 us (94%)
  local copies, waits for them, and re-layouts  2.74 us (4%)
  between operations  0.64 us (1%)
    pallas_call x1, Pallas kernels, fused_shards(): pl.pallas_call(functools.partial(fused_kernel, dims), out_shape=(jax.Shap...  57.3 us
    unnamed x2, local copies, waits for them, and re-layouts  2.74 us

profile of v3, /device:TPU:0, one launch (start us, length us, event | category | flops | bytes accessed | tf_op | source)
XLA Modules:
  0.0 60.7 jit_solution(5078025687073625887)
XLA Ops:
  0.6 57.3 %attend_ffn.1 = (bf16[2,2,2048]{2,1,0:T(2,128)(2,1)}, bf16[1,8192]{1,0:T(2,128)(2,1)}) custom-call(bf16[64,128]{1,0:T(8,128)(2,1)} %bitcast.3, s32[2,2,1,32]{3,2,1,0:T(1,128)} %ids_ref.1, s32[2,2]{1,0:T(2,128)} %fill_ref.1, bf16[2,3,1,2,128]{4,3,2,1,0:T(2,128)(2,1)} %new_ref.1, bf16[2,2,2048]{2,1,0:T(2,128)(2,1)} %resid_ref.1, f32[64,128]{1,0:T(8,128)} %bitcast.2, ...), custom_call_target="tpu_custom_call" | custom-call | tf_op jit(solution)/shard_map/attend_ffn/pallas_call | solution.py:668
  57.9 1.3 %copy.14 = bf16[2,2,2048]{2,1,0:T(2,128)(2,1)} copy(bf16[2,2,2048]{2,1,0:T(2,128)(2,1)} %get-tuple-element.4) | data formatting | bytes 32768
  59.3 1.4 %copy.15 = bf16[1,8192]{1,0:T(2,128)(2,1)} copy(bf16[1,8192]{1,0:T(2,128)(2,1)} %get-tuple-element.5) | data formatting | bytes 32768
